TPU v7x, 32 devices: a whole 2x2x4 slice. The times are simulated.
32 devices in a mesh: expert: 8 (over z, x), dp: 4 (over y, core).
Axes of the slice: x: 2, y: 2, z: 4, core: 2. Of those that a mesh axis runs over, the one named last changes fastest.
Arguments:
- tokens: bfloat16 [2048, 2048], P('expert'), may hold values from -6 to 6
- cotangent: bfloat16 [2048, 2048], P('expert'), may hold values from -6 to 6
- expert_route: int32 [2048, 1], P('expert'), may hold values from 0 to 7; in each aligned block of 256 rows (0 to 255, 256 to 511, ...) at most 64 rows name the same one
- w_gate: bfloat16 [8, 2048, 7168], P('expert', None, 'dp'), may hold values from -0.125 to 0.125
- w_up: bfloat16 [8, 2048, 7168], P('expert', None, 'dp'), may hold values from -0.125 to 0.125
- w_down: bfloat16 [8, 7168, 2048], P('expert', 'dp'), may hold values from -0.0625 to 0.0625
- sign_seeds: int32 [8], P('expert'), may hold values from 0 to 65535
Outputs:
- tangent_grad: bfloat16 [2048, 2048], P('expert')
- curvature: float32 [8, 7168], P('expert', 'dp')
Inputs may be any that keep to these rules, and one draw needn't show every extreme that they name: `expert_route`: among the tokens of one index of expert no expert is named more than 64 times, and in some index one expert is named exactly 64 times; every expert is named by some token.
All inputs are finite; a program needn't handle non-finite values.
Results may differ from a plain program's by a relative error of at most 0.005.
Values may be sent and summed in bfloat16 or wider, within the bound.
A program may use at most 128 MiB of HBM per device.

v0:
```python
import functools
import math

import jax
import jax.numpy as jnp
import ml_dtypes
from jax import lax
from jax.experimental import pallas as pl
from jax.experimental.pallas import tpu as pltpu
from jax.sharding import PartitionSpec as P

MESH = pl.DeviceIdType.MESH
CORES = 2
LAG = 2
NT = (((1,), (1,)), ((), ()))


def loop(low, high, fn):
    def step(index, carry):
        fn(index)
        return carry

    lax.fori_loop(low, high, step, 0)


def kernel(
    cfg,
    route_col, route_row, seed, tok, cot, wg_hbm, wu_hbm, wd_hbm,
    out_hbm, curv,
    wg, wu, wd, sign, base, disp, disp_t, tq, sb, xb, pre, lin, dpre, tgate, tup, ggate,
    ksend, krecv, ysend, yrecv, fin, ret, ob,
    w_sem, t_sem, out_sem, a_send, a_recv, y_send, y_recv, c_send, c_recv,
    k_send, k_recv, p_send, p_recv, b_send, b_recv, oy_send, oy_recv, oc_send, oc_recv,
):
    experts, dps, toks, width, hidden, slots, fc, qw, ch = cfg
    ys = dps // CORES
    rounds = qw // ch
    chunks = hidden // fc
    rows = experts * slots
    me = lax.axis_index("expert")
    mine = lax.axis_index("dp")
    core = lax.rem(mine, CORES)
    y = lax.div(mine, CORES)
    sibling = (me, y * CORES + 1 - core)

    def expert_at(k):
        return lax.rem(me + k, experts)

    def expert_from(k):
        return lax.rem(me - k + experts, experts)

    def y_at(dy):
        return lax.rem(y + dy, ys)

    def y_from(dy):
        return lax.rem(y - dy + ys, ys)

    def y_peer(dy):
        return (me, y_at(dy) * CORES + core)

    def row_block(e):
        return pl.ds(pl.multiple_of(e * slots, slots), slots)

    def quarter(d):
        return pl.ds(pl.multiple_of(d * qw, qw), qw)

    def remote(src, dst, s, r, dev):
        return pltpu.make_async_remote_copy(
            src_ref=src, dst_ref=dst, send_sem=s, recv_sem=r, device_id=dev, device_id_type=MESH
        )

    tok_loads = [
        pltpu.make_async_copy(ref.at[:, quarter(mine)], tq.at[i], t_sem.at[i])
        for i, ref in enumerate((tok, cot))
    ]
    for load in tok_loads:
        load.start()
    w_loads = [
        pltpu.make_async_copy(src.at[0], dst, w_sem.at[i])
        for i, (src, dst) in enumerate(((wg_hbm, wg), (wu_hbm, wu), (wd_hbm, wd)))
    ]
    for load in w_loads:
        load.start()

    barrier = pltpu.get_barrier_semaphore()
    loop(1, experts, lambda k: pl.semaphore_signal(
        barrier, inc=1, device_id=(expert_at(k), mine), device_id_type=MESH))
    loop(1, ys, lambda dy: pl.semaphore_signal(
        barrier, inc=1, device_id=y_peer(dy), device_id_type=MESH))
    pl.semaphore_signal(barrier, inc=1, device_id=sibling, device_id_type=MESH)

    def iota(shape, dim):
        return lax.broadcasted_iota(jnp.int32, shape, dim)

    def ones_where(cond):
        return jnp.where(cond, 1.0, 0.0).astype(jnp.float32)

    pad = max(16, experts)
    hot = ones_where(iota((pad, toks), 0) == route_row[...])
    upper = ones_where(iota((toks, toks), 0) <= iota((toks, toks), 1)).astype(jnp.bfloat16)
    seen = jnp.dot(hot.astype(jnp.bfloat16), upper, preferred_element_type=jnp.float32)
    place = jnp.sum(seen * hot, axis=0, keepdims=True) - 1.0
    target = route_row[...] * slots + place.astype(jnp.int32)
    disp[...] = ones_where(iota((rows, toks), 0) == target).astype(jnp.bfloat16)

    def a_copy(i, k):
        e = expert_at(k)
        return remote(sb.at[i, row_block(e), :], xb.at[i, row_block(me), quarter(mine)],
                      a_send.at[i, k], a_recv.at[i, k], (e, mine))

    def a_landed(i, k):
        spot = xb.at[i, row_block(expert_from(k)), quarter(mine)]
        return remote(spot, spot, a_send.at[i, k], a_recv.at[i, k], (expert_from(k), mine))

    def y_copy(i, dy, k):
        spot = xb.at[i, row_block(expert_from(k)), quarter(mine)]
        return remote(spot, spot, y_send.at[i, dy, k], y_recv.at[i, dy, k], y_peer(dy))

    def c_copy(i, dy, k):
        d = y_from(dy) * CORES + core
        spot = xb.at[i, row_block(expert_from(k)), quarter(d)]
        return remote(spot, spot, c_send.at[i, dy, k], c_recv.at[i, dy, k], sibling)

    def y_landed(i, dy, k):
        d = y_from(dy) * CORES + core
        spot = xb.at[i, row_block(expert_from(k)), quarter(d)]
        return remote(spot, spot, y_send.at[i, dy, k], y_recv.at[i, dy, k], y_peer(dy))

    def c_landed(i, dy, k):
        d = y_from(dy) * CORES + 1 - core
        spot = xb.at[i, row_block(expert_from(k)), quarter(d)]
        return remote(spot, spot, c_send.at[i, dy, k], c_recv.at[i, dy, k], sibling)

    def dispatch(i):
        tok_loads[i].wait()
        sb[i] = jnp.dot(disp[...], tq[i], preferred_element_type=jnp.float32).astype(jnp.bfloat16)

    def keep_own(i):
        xb[i, row_block(me), quarter(mine)] = sb[i, row_block(me), :]

    def forward(i, k):
        @pl.when(k > 0)
        def _():
            a_landed(i, k).wait_recv()

        loop(1, ys, lambda dy: y_copy(i, dy, k).start())
        c_copy(i, 0, k).start()

    def second_hop(i, k):
        def one(dy):
            y_landed(i, dy, k).wait_recv()
            c_copy(i, dy, k).start()

        loop(1, ys, one)

    def all_landed(i):
        loop(0, experts, lambda k: loop(0, ys, lambda dy: c_landed(i, dy, k).wait_recv()))

    dispatch(0)
    keep_own(0)
    pl.semaphore_wait(barrier, experts - 1 + ys)
    loop(1, experts, lambda k: a_copy(0, k).start())
    dispatch(1)
    keep_own(1)

    hot_t = ones_where(iota((toks, 128), 1) == route_col[...])
    lower = ones_where(iota((toks, toks), 0) >= iota((toks, toks), 1)).astype(jnp.bfloat16)
    seen_t = jnp.dot(lower, hot_t.astype(jnp.bfloat16), preferred_element_type=jnp.float32)
    place_t = jnp.sum(seen_t * hot_t, axis=1, keepdims=True) - 1.0
    target_t = route_col[...] * slots + place_t.astype(jnp.int32)
    disp_t[...] = ones_where(iota((toks, rows), 1) == target_t).astype(jnp.bfloat16)

    scale = float(ml_dtypes.bfloat16(1.0 / math.sqrt(width)))
    band = 16
    base[...] = (
        iota((band, hidden), 0) * 73856093
        + (iota((band, hidden), 1) + mine * hidden) * 19349663
        + seed[0] * 83492791
    )

    def sign_rows(row0):
        m = base[...] + row0 * 73856093
        m = m ^ (m >> 15)
        m = m * 735632791
        m = m ^ (m >> 13)
        m = m * 1274126177
        m = m ^ (m >> 16)
        sign[pl.ds(pl.multiple_of(row0, band), band), :] = jnp.where(
            (m & 32) != 0, scale, -scale).astype(jnp.bfloat16)

    part = width // experts

    def first_steps(k):
        forward(0, k)

        @pl.when(k > 0)
        def _():
            a_copy(1, k).start()

        @pl.when(k >= LAG)
        def _():
            second_hop(0, k - LAG)

        loop(0, part // band, lambda j: sign_rows(k * part + j * band))

    loop(0, experts, first_steps)
    loop(experts - LAG, experts, lambda k: second_hop(0, k))
    w_loads[0].wait()
    w_loads[1].wait()
    all_landed(0)

    def cols(c):
        return pl.ds(pl.multiple_of(c * fc, fc), fc)

    def first_dots(c):
        forward(1, c)

        @pl.when(c >= LAG)
        def _():
            second_hop(1, c - LAG)

        x = xb[0]
        pre[c] = jnp.dot(x, wg[:, cols(c)], preferred_element_type=jnp.float32)
        lin[c] = jnp.dot(x, wu[:, cols(c)], preferred_element_type=jnp.float32)
        dpre[c] = jnp.dot(x, sign[:, cols(c)], preferred_element_type=jnp.float32)

    early = min(chunks, experts)
    loop(0, early, first_dots)
    loop(early, experts, lambda k: forward(1, k))
    loop(early - LAG, experts, lambda k: second_hop(1, k))
    w_loads[2].wait()
    all_landed(1)

    def gates(c):
        hgrad = lax.dot_general(xb[1], wd[cols(c), :], NT, preferred_element_type=jnp.float32)
        p, up, tangent = pre[c], lin[c], dpre[c]
        sig = jax.nn.sigmoid(p)
        slope = sig * (1.0 + p * (1.0 - sig))
        bend = sig * (1.0 - sig) * (2.0 + p * (1.0 - 2.0 * sig))
        both = hgrad * up
        tg = both * bend * tangent
        ggate[:, cols(c)] = (both * slope).astype(jnp.bfloat16)
        tup[:, cols(c)] = (hgrad * slope * tangent).astype(jnp.bfloat16)
        tgate[:, cols(c)] = tg.astype(jnp.bfloat16)
        curv[:, cols(c)] = jnp.sum(tangent * tg, axis=0, keepdims=True)

    loop(0, chunks, gates)

    def out_chunk(d, r):
        at = pl.ds(pl.multiple_of(d * qw + r * ch, ch), ch)
        total = lax.dot_general(tgate[...], wg[at, :], NT, preferred_element_type=jnp.float32)
        total += lax.dot_general(tup[...], wu[at, :], NT, preferred_element_type=jnp.float32)
        total += lax.dot_general(ggate[...], sign[at, :], NT, preferred_element_type=jnp.float32)
        return total

    def k_copy(dy, r):
        return remote(ksend.at[dy, r], krecv.at[dy, r], k_send.at[dy, r], k_recv.at[dy, r], sibling)

    def p_copy(dy, r):
        return remote(ysend.at[dy, r], yrecv.at[dy, r], p_send.at[dy, r], p_recv.at[dy, r], y_peer(dy))

    def b_copy(r, k):
        e = expert_at(k)
        return remote(fin.at[r, row_block(e), :], ret.at[r, row_block(me), :],
                      b_send.at[r, k], b_recv.at[r, k], (e, mine))

    def b_landed(r, k):
        spot = ret.at[r, row_block(expert_from(k)), :]
        return remote(spot, spot, b_send.at[r, k], b_recv.at[r, k], (expert_from(k), mine))

    def pair_sum(dy, r):
        ksend[dy, r] = out_chunk(y_at(dy) * CORES + 1 - core, r).astype(jnp.bfloat16)
        k_copy(dy, r).start()
        own = out_chunk(y_at(dy) * CORES + core, r)
        k_copy(dy, r).wait_recv()
        return own + krecv[dy, r].astype(jnp.float32)

    def far(step):
        dy, r = 1 + lax.div(step, rounds), lax.rem(step, rounds)
        ysend[dy, r] = pair_sum(dy, r).astype(jnp.bfloat16)
        p_copy(dy, r).start()

    def near(r):
        total = pair_sum(0, r)
        for dy in range(1, ys):
            p_copy(dy, r).wait_recv()
            total += yrecv[dy, r].astype(jnp.float32)
        fin[r] = total.astype(jnp.bfloat16)
        loop(1, experts, lambda k: b_copy(r, k).start())
        ret[r, row_block(me), :] = fin[r, row_block(me), :]

    loop(0, (ys - 1) * rounds, far)
    loop(0, rounds, near)

    def o_spot(d, r):
        return ob.at[:, pl.ds(pl.multiple_of(d * qw + r * ch, ch), ch)]

    def oy_copy(dy, r):
        spot = o_spot(mine, r)
        return remote(spot, spot, oy_send.at[dy, r], oy_recv.at[dy, r], y_peer(dy))

    def oy_landed(dy, r):
        spot = o_spot(y_from(dy) * CORES + core, r)
        return remote(spot, spot, oy_send.at[dy, r], oy_recv.at[dy, r], y_peer(dy))

    def oc_copy(dy, r):
        spot = o_spot(y_from(dy) * CORES + core, r)
        return remote(spot, spot, oc_send.at[dy, r], oc_recv.at[dy, r], sibling)

    def oc_landed(dy, r):
        spot = o_spot(y_from(dy) * CORES + 1 - core, r)
        return remote(spot, spot, oc_send.at[dy, r], oc_recv.at[dy, r], sibling)

    def combine(r):
        loop(1, experts, lambda k: b_landed(r, k).wait_recv())
        ob[:, pl.ds(pl.multiple_of(mine * qw + r * ch, ch), ch)] = jnp.dot(
            disp_t[...], ret[r], preferred_element_type=jnp.float32).astype(jnp.bfloat16)
        loop(1, ys, lambda dy: oy_copy(dy, r).start())
        oc_copy(0, r).start()

    loop(0, rounds, combine)

    def out_hop(r):
        def one(dy):
            oy_landed(dy, r).wait_recv()
            oc_copy(dy, r).start()

        loop(1, ys, one)

    loop(0, rounds, out_hop)
    loop(0, rounds, lambda r: loop(0, ys, lambda dy: oc_landed(dy, r).wait_recv()))
    write = pltpu.make_async_copy(ob, out_hbm, out_sem)
    write.start()

    def drain(i):
        def one(k):
            @pl.when(k > 0)
            def _():
                a_copy(i, k).wait_send()

            loop(1, ys, lambda dy: y_copy(i, dy, k).wait_send())
            loop(0, ys, lambda dy: c_copy(i, dy, k).wait_send())

        loop(0, experts, one)

    loop(0, 2, drain)

    def drain_out(r):
        loop(0, ys, lambda dy: k_copy(dy, r).wait_send())
        loop(1, ys, lambda dy: p_copy(dy, r).wait_send())
        loop(1, experts, lambda k: b_copy(r, k).wait_send())
        loop(1, ys, lambda dy: oy_copy(dy, r).wait_send())
        loop(0, ys, lambda dy: oc_copy(dy, r).wait_send())

    loop(0, rounds, drain_out)
    write.wait()


def body(tokens, cotangent, expert_route, w_gate, w_up, w_down, sign_seeds):
    experts = lax.axis_size("expert")
    dps = lax.axis_size("dp")
    toks, width = tokens.shape
    hidden = w_gate.shape[2]
    slots = max(2, 2 * toks // experts)
    rows = experts * slots
    ys = dps // CORES
    qw = width // dps
    ch = min(256, qw)
    rounds = qw // ch
    fc = 256 if hidden % 256 == 0 else 128
    chunks = hidden // fc
    cfg = (experts, dps, toks, width, hidden, slots, fc, qw, ch)
    bf, f32 = jnp.bfloat16, jnp.float32
    vm, dma = pltpu.VMEM, pltpu.SemaphoreType.DMA
    anywhere = pl.BlockSpec(memory_space=pl.ANY)
    in_vmem = pl.BlockSpec(memory_space=pltpu.VMEM)
    return pl.pallas_call(
        functools.partial(kernel, cfg),
        out_shape=(
            jax.ShapeDtypeStruct((toks, width), bf),
            jax.ShapeDtypeStruct((1, hidden), f32),
        ),
        in_specs=[in_vmem, in_vmem, pl.BlockSpec(memory_space=pltpu.SMEM)] + [anywhere] * 5,
        out_specs=(anywhere, in_vmem),
        scratch_shapes=[
            vm((width, hidden), bf), vm((width, hidden), bf), vm((hidden, width), bf),
            vm((width, hidden), bf), vm((16, hidden), jnp.int32),
            vm((rows, toks), bf), vm((toks, rows), bf),
            vm((2, toks, qw), bf), vm((2, rows, qw), bf), vm((2, rows, width), bf),
            vm((chunks, rows, fc), f32), vm((chunks, rows, fc), f32), vm((chunks, rows, fc), f32),
            vm((rows, hidden), bf), vm((rows, hidden), bf), vm((rows, hidden), bf),
            vm((ys, rounds, rows, ch), bf), vm((ys, rounds, rows, ch), bf),
            vm((ys, rounds, rows, ch), bf), vm((ys, rounds, rows, ch), bf),
            vm((rounds, rows, ch), bf), vm((rounds, rows, ch), bf),
            vm((toks, width), bf),
            dma((3,)), dma((2,)), dma,
            dma((2, experts)), dma((2, experts)),
            dma((2, ys, experts)), dma((2, ys, experts)),
            dma((2, ys, experts)), dma((2, ys, experts)),
            dma((ys, rounds)), dma((ys, rounds)),
            dma((ys, rounds)), dma((ys, rounds)),
            dma((rounds, experts)), dma((rounds, experts)),
            dma((ys, rounds)), dma((ys, rounds)),
            dma((ys, rounds)), dma((ys, rounds)),
        ],
        compiler_params=pltpu.CompilerParams(
            collective_id=0, has_side_effects=True, vmem_limit_bytes=63 * 1024 * 1024
        ),
    )(
        expert_route, expert_route.reshape(1, toks), sign_seeds,
        tokens, cotangent, w_gate, w_up, w_down,
    )


def solution(mesh):
    in_specs = (
        P("expert", None),
        P("expert", None),
        P("expert", None),
        P("expert", None, "dp"),
        P("expert", None, "dp"),
        P("expert", "dp", None),
        P("expert"),
    )
    out_specs = (P("expert", None), P("expert", "dp"))
    return jax.shard_map(body, mesh=mesh, in_specs=in_specs, out_specs=out_specs, check_vma=False)
```

profile of v0, /device:TPU:1, one launch (start us, length us, event | category | flops | bytes accessed | tf_op | source)
XLA Modules:
  0.0 103.5 jit_solution(1216136826635105603)
XLA Ops:
  1.3 1.5 %copy.9.route_col = s32[256,1]{1,0:T(8,128)} copy(s32[256,1]{0,1:T(1,128)} %param.9) | data formatting | bytes 2048 | tf_op args[2]
  2.8 97.1 %shard_map.86 = (bf16[256,2048]{1,0:T(8,128)(2,1)}, f32[1,1792]{1,0:T(1,128)}) custom-call(s32[256,1]{1,0:T(8,128)} %copy.9.route_col, s32[1,256]{1,0:T(1,128)} %bitcast.1, s32[1]{0:T(128)S(6)} %copy.12.seed, bf16[256,2048]{1,0:T(8,128)(2,1)} %tok.1, bf16[256,2048]{1,0:T(8,128)(2,1)} %cot.1, bf16[1,2048,1792]{2,1,0:T(8,128)(2,1)} %wg_hbm.1, ...), custom_call_target="tpu_custom_call" | custom-call | tf_op jit(solution)/shard_map/pallas_call | solution.py:377
  99.9 2.3 %copy.13 = bf16[256,2048]{1,0:T(8,128)(2,1)} copy(bf16[256,2048]{1,0:T(8,128)(2,1)} %get-tuple-element.4) | data formatting | bytes 2097152
  102.2 1.3 %copy.14 = f32[1,1792]{1,0:T(1,128)} copy(f32[1,1792]{1,0:T(1,128)} %get-tuple-element.5) | data formatting | bytes 14336
where the time goes:
time: 104 us; the launch traced here: 103 us
  Pallas kernels  97.1 us (93%)
  local copies, waits for them, and re-layouts  5.07 us (5%)
  between operations  1.29 us (1%)
    pallas_call x1, Pallas kernels, body(): pl.pallas_call(functools.partial(kernel, cfg), out_shape=(jax.ShapeDtypeS...  97.1 us
    unnamed x3, local copies, waits for them, and re-layouts  5.07 us

commit v1 on v0

--- a/solution.py
+++ b/solution.py
@@ -25,10 +25,10 @@
 
 def kernel(
     cfg,
-    route_col, route_row, seed, tok, cot, wg_hbm, wu_hbm, wd_hbm,
+    route_row, seed, tok, cot, wg_hbm, wu_hbm, wd_hbm,
     out_hbm, curv,
-    wg, wu, wd, sign, base, disp, disp_t, tq, sb, xb, pre, lin, dpre, tgate, tup, ggate,
-    ksend, krecv, ysend, yrecv, fin, ret, ob,
+    w3, wd, base, disp, disp_t, tq, sb, xb, first, h3,
+    ksend, krecv, own, ysend, yrecv, fin, ret, ob,
     w_sem, t_sem, out_sem, a_send, a_recv, y_send, y_recv, c_send, c_recv,
     k_send, k_recv, p_send, p_recv, b_send, b_recv, oy_send, oy_recv, oc_send, oc_recv,
 ):
@@ -76,9 +76,13 @@
     for load in tok_loads:
         load.start()
     w_loads = [
-        pltpu.make_async_copy(src.at[0], dst, w_sem.at[i])
-        for i, (src, dst) in enumerate(((wg_hbm, wg), (wu_hbm, wu), (wd_hbm, wd)))
+        pltpu.make_async_copy(
+            src.at[0, :, pl.ds(c * fc, fc)], w3.at[:, pl.ds((3 * c + i) * fc, fc)], w_sem.at[i, c]
+        )
+        for c in range(chunks)
+        for i, src in enumerate((wg_hbm, wu_hbm))
     ]
+    w_loads.append(pltpu.make_async_copy(wd_hbm.at[0], wd, w_sem.at[2, 0]))
     for load in w_loads:
         load.start()
 
@@ -101,7 +105,8 @@
     seen = jnp.dot(hot.astype(jnp.bfloat16), upper, preferred_element_type=jnp.float32)
     place = jnp.sum(seen * hot, axis=0, keepdims=True) - 1.0
     target = route_row[...] * slots + place.astype(jnp.int32)
-    disp[...] = ones_where(iota((rows, toks), 0) == target).astype(jnp.bfloat16)
+    spots = ones_where(iota((rows, toks), 0) == target)
+    disp[...] = spots.astype(jnp.bfloat16)
 
     def a_copy(i, k):
         e = expert_at(k)
@@ -163,12 +168,7 @@
     dispatch(1)
     keep_own(1)
 
-    hot_t = ones_where(iota((toks, 128), 1) == route_col[...])
-    lower = ones_where(iota((toks, toks), 0) >= iota((toks, toks), 1)).astype(jnp.bfloat16)
-    seen_t = jnp.dot(lower, hot_t.astype(jnp.bfloat16), preferred_element_type=jnp.float32)
-    place_t = jnp.sum(seen_t * hot_t, axis=1, keepdims=True) - 1.0
-    target_t = route_col[...] * slots + place_t.astype(jnp.int32)
-    disp_t[...] = ones_where(iota((toks, rows), 1) == target_t).astype(jnp.bfloat16)
+    disp_t[...] = jnp.transpose(spots).astype(jnp.bfloat16)
 
     scale = float(ml_dtypes.bfloat16(1.0 / math.sqrt(width)))
     band = 16
@@ -185,8 +185,10 @@
         m = m ^ (m >> 13)
         m = m * 1274126177
         m = m ^ (m >> 16)
-        sign[pl.ds(pl.multiple_of(row0, band), band), :] = jnp.where(
-            (m & 32) != 0, scale, -scale).astype(jnp.bfloat16)
+        signs = jnp.where((m & 32) != 0, scale, -scale).astype(jnp.bfloat16)
+        for c in range(chunks):
+            w3[pl.ds(pl.multiple_of(row0, band), band), pl.ds((3 * c + 2) * fc, fc)] = (
+                signs[:, c * fc:(c + 1) * fc])
 
     part = width // experts
 
@@ -205,12 +207,9 @@
 
     loop(0, experts, first_steps)
     loop(experts - LAG, experts, lambda k: second_hop(0, k))
-    w_loads[0].wait()
-    w_loads[1].wait()
+    for load in w_loads[:-1]:
+        load.wait()
     all_landed(0)
-
-    def cols(c):
-        return pl.ds(pl.multiple_of(c * fc, fc), fc)
 
     def first_dots(c):
         forward(1, c)
@@ -219,39 +218,46 @@
         def _():
             second_hop(1, c - LAG)
 
-        x = xb[0]
-        pre[c] = jnp.dot(x, wg[:, cols(c)], preferred_element_type=jnp.float32)
-        lin[c] = jnp.dot(x, wu[:, cols(c)], preferred_element_type=jnp.float32)
-        dpre[c] = jnp.dot(x, sign[:, cols(c)], preferred_element_type=jnp.float32)
+        first[c] = jnp.dot(
+            xb[0], w3[:, pl.ds(pl.multiple_of(c * 3 * fc, 3 * fc), 3 * fc)],
+            preferred_element_type=jnp.float32)
 
     early = min(chunks, experts)
     loop(0, early, first_dots)
     loop(early, experts, lambda k: forward(1, k))
     loop(early - LAG, experts, lambda k: second_hop(1, k))
-    w_loads[2].wait()
+    w_loads[-1].wait()
     all_landed(1)
 
-    def gates(c):
-        hgrad = lax.dot_general(xb[1], wd[cols(c), :], NT, preferred_element_type=jnp.float32)
-        p, up, tangent = pre[c], lin[c], dpre[c]
-        sig = jax.nn.sigmoid(p)
-        slope = sig * (1.0 + p * (1.0 - sig))
-        bend = sig * (1.0 - sig) * (2.0 + p * (1.0 - 2.0 * sig))
-        both = hgrad * up
-        tg = both * bend * tangent
-        ggate[:, cols(c)] = (both * slope).astype(jnp.bfloat16)
-        tup[:, cols(c)] = (hgrad * slope * tangent).astype(jnp.bfloat16)
-        tgate[:, cols(c)] = tg.astype(jnp.bfloat16)
-        curv[:, cols(c)] = jnp.sum(tangent * tg, axis=0, keepdims=True)
-
-    loop(0, chunks, gates)
-
-    def out_chunk(d, r):
-        at = pl.ds(pl.multiple_of(d * qw + r * ch, ch), ch)
-        total = lax.dot_general(tgate[...], wg[at, :], NT, preferred_element_type=jnp.float32)
-        total += lax.dot_general(tup[...], wu[at, :], NT, preferred_element_type=jnp.float32)
-        total += lax.dot_general(ggate[...], sign[at, :], NT, preferred_element_type=jnp.float32)
-        return total
+    def gates(c, hgrad):
+        lanes = [pl.ds(i * fc, fc) for i in range(3)]
+        total = jnp.zeros((1, fc), jnp.float32)
+        tall = 32
+        for row in range(0, rows, tall):
+            at = pl.ds(row, tall)
+            hg = hgrad[row:row + tall]
+            p, up, tangent = (first[c, at, lane] for lane in lanes)
+            sig = jax.nn.sigmoid(p)
+            slope = sig * (1.0 + p * (1.0 - sig))
+            bend = sig * (1.0 - sig) * (2.0 + p * (1.0 - 2.0 * sig))
+            both = hg * up
+            tg = both * bend * tangent
+            parts = (tg, hg * slope * tangent, both * slope)
+            for i, value in enumerate(parts):
+                h3[at, pl.ds((3 * c + i) * fc, fc)] = value.astype(jnp.bfloat16)
+            total += jnp.sum(tangent * tg, axis=0, keepdims=True)
+        curv[:, pl.ds(c * fc, fc)] = total
+
+    for c in range(0, chunks, 2):
+        n = min(2, chunks - c)
+        hgrads = lax.dot_general(
+            xb[1], wd[pl.ds(c * fc, n * fc), :], NT, preferred_element_type=jnp.float32)
+        for i in range(n):
+            gates(c + i, hgrads[:, i * fc:(i + 1) * fc])
+
+    def block_at(d, r):
+        index = (lax.div(d, CORES) * rounds + r) * CORES + lax.rem(d, CORES)
+        return pl.multiple_of(index * ch, ch)
 
     def k_copy(dy, r):
         return remote(ksend.at[dy, r], krecv.at[dy, r], k_send.at[dy, r], k_recv.at[dy, r], sibling)
@@ -268,32 +274,49 @@
         spot = ret.at[r, row_block(expert_from(k)), :]
         return remote(spot, spot, b_send.at[r, k], b_recv.at[r, k], (expert_from(k), mine))
 
-    def pair_sum(dy, r):
-        ksend[dy, r] = out_chunk(y_at(dy) * CORES + 1 - core, r).astype(jnp.bfloat16)
+    def split(step):
+        return lax.rem(1 + lax.div(step, rounds), ys), lax.rem(step, rounds)
+
+    def multiply(step):
+        dy, r = split(step)
+        at = pl.ds(pl.multiple_of((y_at(dy) * rounds + r) * CORES * ch, CORES * ch), CORES * ch)
+        pair = lax.dot_general(h3[...], w3[at, :], NT, preferred_element_type=jnp.float32)
+        left, right = pair[:, :ch], pair[:, ch:]
+        ksend[dy, r] = jnp.where(core == 0, right, left).astype(jnp.bfloat16)
         k_copy(dy, r).start()
-        own = out_chunk(y_at(dy) * CORES + core, r)
+        own[dy, r] = jnp.where(core == 0, left, right)
+
+    def finish(step):
+        dy, r = split(step)
         k_copy(dy, r).wait_recv()
-        return own + krecv[dy, r].astype(jnp.float32)
-
-    def far(step):
-        dy, r = 1 + lax.div(step, rounds), lax.rem(step, rounds)
-        ysend[dy, r] = pair_sum(dy, r).astype(jnp.bfloat16)
-        p_copy(dy, r).start()
-
-    def near(r):
-        total = pair_sum(0, r)
-        for dy in range(1, ys):
-            p_copy(dy, r).wait_recv()
-            total += yrecv[dy, r].astype(jnp.float32)
-        fin[r] = total.astype(jnp.bfloat16)
-        loop(1, experts, lambda k: b_copy(r, k).start())
-        ret[r, row_block(me), :] = fin[r, row_block(me), :]
-
-    loop(0, (ys - 1) * rounds, far)
-    loop(0, rounds, near)
+
+        @pl.when(dy > 0)
+        def _():
+            ysend[dy, r] = (own[dy, r] + krecv[dy, r].astype(jnp.float32)).astype(jnp.bfloat16)
+            p_copy(dy, r).start()
+
+        @pl.when(dy == 0)
+        def _():
+            total = own[0, r] + krecv[0, r].astype(jnp.float32)
+            for other in range(1, ys):
+                p_copy(other, r).wait_recv()
+                total += yrecv[other, r].astype(jnp.float32)
+            fin[r] = total.astype(jnp.bfloat16)
+            loop(1, experts, lambda k: b_copy(r, k).start())
+            ret[r, row_block(me), :] = fin[r, row_block(me), :]
+
+    def both_steps(step):
+        multiply(step)
+
+        @pl.when(step > 0)
+        def _():
+            finish(step - 1)
+
+    loop(0, ys * rounds, both_steps)
+    finish(ys * rounds - 1)
 
     def o_spot(d, r):
-        return ob.at[:, pl.ds(pl.multiple_of(d * qw + r * ch, ch), ch)]
+        return ob.at[:, pl.ds(block_at(d, r), ch)]
 
     def oy_copy(dy, r):
         spot = o_spot(mine, r)
@@ -313,7 +336,7 @@
 
     def combine(r):
         loop(1, experts, lambda k: b_landed(r, k).wait_recv())
-        ob[:, pl.ds(pl.multiple_of(mine * qw + r * ch, ch), ch)] = jnp.dot(
+        ob[:, pl.ds(block_at(mine, r), ch)] = jnp.dot(
             disp_t[...], ret[r], preferred_element_type=jnp.float32).astype(jnp.bfloat16)
         loop(1, ys, lambda dy: oy_copy(dy, r).start())
         oc_copy(0, r).start()
@@ -380,20 +403,19 @@
             jax.ShapeDtypeStruct((toks, width), bf),
             jax.ShapeDtypeStruct((1, hidden), f32),
         ),
-        in_specs=[in_vmem, in_vmem, pl.BlockSpec(memory_space=pltpu.SMEM)] + [anywhere] * 5,
+        in_specs=[in_vmem, pl.BlockSpec(memory_space=pltpu.SMEM)] + [anywhere] * 5,
         out_specs=(anywhere, in_vmem),
         scratch_shapes=[
-            vm((width, hidden), bf), vm((width, hidden), bf), vm((hidden, width), bf),
-            vm((width, hidden), bf), vm((16, hidden), jnp.int32),
+            vm((width, 3 * hidden), bf), vm((hidden, width), bf), vm((16, hidden), jnp.int32),
             vm((rows, toks), bf), vm((toks, rows), bf),
             vm((2, toks, qw), bf), vm((2, rows, qw), bf), vm((2, rows, width), bf),
-            vm((chunks, rows, fc), f32), vm((chunks, rows, fc), f32), vm((chunks, rows, fc), f32),
-            vm((rows, hidden), bf), vm((rows, hidden), bf), vm((rows, hidden), bf),
+            vm((chunks, rows, 3 * fc), f32), vm((rows, 3 * hidden), bf),
             vm((ys, rounds, rows, ch), bf), vm((ys, rounds, rows, ch), bf),
+            vm((ys, rounds, rows, ch), f32),
             vm((ys, rounds, rows, ch), bf), vm((ys, rounds, rows, ch), bf),
             vm((rounds, rows, ch), bf), vm((rounds, rows, ch), bf),
             vm((toks, width), bf),
-            dma((3,)), dma((2,)), dma,
+            dma((3, chunks)), dma((2,)), dma,
             dma((2, experts)), dma((2, experts)),
             dma((2, ys, experts)), dma((2, ys, experts)),
             dma((2, ys, experts)), dma((2, ys, experts)),
@@ -407,7 +429,7 @@
             collective_id=0, has_side_effects=True, vmem_limit_bytes=63 * 1024 * 1024
         ),
     )(
-        expert_route, expert_route.reshape(1, toks), sign_seeds,
+        expert_route.reshape(1, toks), sign_seeds,
         tokens, cotangent, w_gate, w_up, w_down,
     )
 

time: 104 us -> 98.6 us (0.948)
  Pallas kernels: 97.1 us -> 93.5 us
  local copies, waits for them, and re-layouts: 5.07 us -> 3.59 us
    pallas_call x1, Pallas kernels: 97.1 us -> 93.5 us  [body(): pl.pallas_call(functools.partial(kernel, cfg), out_shape=(jax.ShapeDtypeS...]
    unnamed x3 -> x2, local copies, waits for them, and re-layouts: 5.07 us -> 3.59 us
where the time goes in v1:
time: 98.6 us; the launch traced here: 98.4 us
  Pallas kernels  93.5 us (95%)
  local copies, waits for them, and re-layouts  3.59 us (4%)
  between operations  1.29 us (1%)
    pallas_call x1, Pallas kernels, body(): pl.pallas_call(functools.partial(kernel, cfg), out_shape=(jax.ShapeDtypeS...  93.5 us
    unnamed x2, local copies, waits for them, and re-layouts  3.59 us

profile of v1, /device:TPU:1, one launch (start us, length us, event | category | flops | bytes accessed | tf_op | source)
XLA Modules:
  0.0 98.4 jit_solution(7342128622717511647)
XLA Ops:
  1.3 93.5 %shard_map.86 = (bf16[256,2048]{1,0:T(8,128)(2,1)}, f32[1,1792]{1,0:T(1,128)}) custom-call(s32[1,256]{1,0:T(1,128)} %bitcast.1, s32[1]{0:T(128)S(6)} %copy.11.seed, bf16[256,2048]{1,0:T(8,128)(2,1)} %tok.1, bf16[256,2048]{1,0:T(8,128)(2,1)} %cot.1, bf16[1,2048,1792]{2,1,0:T(8,128)(2,1)} %wg_hbm.1, bf16[1,2048,1792]{2,1,0:T(8,128)(2,1)} %wu_hbm.1, ...), custom_call_target="tpu_custom_call" | custom-call | tf_op jit(solution)/shard_map/pallas_call | solution.py:400
  94.8 2.3 %copy.12 = bf16[256,2048]{1,0:T(8,128)(2,1)} copy(bf16[256,2048]{1,0:T(8,128)(2,1)} %get-tuple-element.4) | data formatting | bytes 2097152
  97.1 1.3 %copy.13 = f32[1,1792]{1,0:T(1,128)} copy(f32[1,1792]{1,0:T(1,128)} %get-tuple-element.5) | data formatting | bytes 14336

commit v2 on v1

--- a/solution.py
+++ b/solution.py
@@ -12,6 +12,7 @@
 MESH = pl.DeviceIdType.MESH
 CORES = 2
 LAG = 2
+WINDOW = 3
 NT = (((1,), (1,)), ((), ()))
 
 
@@ -37,6 +38,7 @@
     rounds = qw // ch
     chunks = hidden // fc
     rows = experts * slots
+    window = min(WINDOW, experts - 1)
     me = lax.axis_index("expert")
     mine = lax.axis_index("dp")
     core = lax.rem(mine, CORES)
@@ -143,10 +145,24 @@
     def keep_own(i):
         xb[i, row_block(me), quarter(mine)] = sb[i, row_block(me), :]
 
+    def send_next(i, k):
+        later = k + window
+
+        @pl.when((later < experts) & (k > (0 if i else -1)))
+        def _():
+            a_copy(i, later).start()
+
+        if i == 0:
+            @pl.when(later >= experts)
+            def _():
+                a_copy(1, later - experts + 1).start()
+
     def forward(i, k):
         @pl.when(k > 0)
         def _():
             a_landed(i, k).wait_recv()
+
+        send_next(i, k)
 
         loop(1, ys, lambda dy: y_copy(i, dy, k).start())
         c_copy(i, 0, k).start()
@@ -164,7 +180,7 @@
     dispatch(0)
     keep_own(0)
     pl.semaphore_wait(barrier, experts - 1 + ys)
-    loop(1, experts, lambda k: a_copy(0, k).start())
+    loop(1, window, lambda k: a_copy(0, k).start())
     dispatch(1)
     keep_own(1)
 
@@ -194,10 +210,6 @@
 
     def first_steps(k):
         forward(0, k)
-
-        @pl.when(k > 0)
-        def _():
-            a_copy(1, k).start()
 
         @pl.when(k >= LAG)
         def _():

time: 98.6 us -> 95 us (0.963)
  Pallas kernels: 93.5 us -> 89.9 us
    pallas_call x1, Pallas kernels: 93.5 us -> 89.9 us  [body(): pl.pallas_call(functools.partial(kernel, cfg), out_shape=(jax.ShapeDtypeS...]
where the time goes in v2:
time: 95 us; the launch traced here: 94.8 us
  Pallas kernels  89.9 us (95%)
  local copies, waits for them, and re-layouts  3.59 us (4%)
  between operations  1.29 us (1%)
    pallas_call x1, Pallas kernels, body(): pl.pallas_call(functools.partial(kernel, cfg), out_shape=(jax.ShapeDtypeS...  89.9 us
    unnamed x2, local copies, waits for them, and re-layouts  3.59 us

profile of v2, /device:TPU:1, one launch (start us, length us, event | category | flops | bytes accessed | tf_op | source)
XLA Modules:
  0.0 94.8 jit_solution(8980972443115757575)
XLA Ops:
  1.3 89.9 %shard_map.86 = (bf16[256,2048]{1,0:T(8,128)(2,1)}, f32[1,1792]{1,0:T(1,128)}) custom-call(s32[1,256]{1,0:T(1,128)} %bitcast.1, s32[1]{0:T(128)S(6)} %copy.11.seed, bf16[256,2048]{1,0:T(8,128)(2,1)} %tok.1, bf16[256,2048]{1,0:T(8,128)(2,1)} %cot.1, bf16[1,2048,1792]{2,1,0:T(8,128)(2,1)} %wg_hbm.1, bf16[1,2048,1792]{2,1,0:T(8,128)(2,1)} %wu_hbm.1, ...), custom_call_target="tpu_custom_call" | custom-call | tf_op jit(solution)/shard_map/pallas_call | solution.py:412
  91.2 2.3 %copy.12 = bf16[256,2048]{1,0:T(8,128)(2,1)} copy(bf16[256,2048]{1,0:T(8,128)(2,1)} %get-tuple-element.4) | data formatting | bytes 2097152
  93.5 1.3 %copy.13 = f32[1,1792]{1,0:T(1,128)} copy(f32[1,1792]{1,0:T(1,128)} %get-tuple-element.5) | data formatting | bytes 14336

commit v3 on v2

--- a/solution.py
+++ b/solution.py
@@ -400,7 +400,7 @@
     rows = experts * slots
     ys = dps // CORES
     qw = width // dps
-    ch = min(256, qw)
+    ch = min(128, qw)
     rounds = qw // ch
     fc = 256 if hidden % 256 == 0 else 128
     chunks = hidden // fc

time: 95 us -> 92.3 us (0.972)
  Pallas kernels: 89.9 us -> 87.2 us
    pallas_call x1, Pallas kernels: 89.9 us -> 87.2 us  [body(): pl.pallas_call(functools.partial(kernel, cfg), out_shape=(jax.ShapeDtypeS...]
where the time goes in v3:
time: 92.3 us; the launch traced here: 92 us
  Pallas kernels  87.2 us (94%)
  local copies, waits for them, and re-layouts  3.59 us (4%)
  between operations  1.29 us (1%)
    pallas_call x1, Pallas kernels, body(): pl.pallas_call(functools.partial(kernel, cfg), out_shape=(jax.ShapeDtypeS...  87.2 us
    unnamed x2, local copies, waits for them, and re-layouts  3.59 us

profile of v3, /device:TPU:1, one launch (start us, length us, event | category | flops | bytes accessed | tf_op | source)
XLA Modules:
  0.0 92.0 jit_solution(725091185902052341)
XLA Ops:
  1.3 87.2 %shard_map.86 = (bf16[256,2048]{1,0:T(8,128)(2,1)}, f32[1,1792]{1,0:T(1,128)}) custom-call(s32[1,256]{1,0:T(1,128)} %bitcast.1, s32[1]{0:T(128)S(6)} %copy.11.seed, bf16[256,2048]{1,0:T(8,128)(2,1)} %tok.1, bf16[256,2048]{1,0:T(8,128)(2,1)} %cot.1, bf16[1,2048,1792]{2,1,0:T(8,128)(2,1)} %wg_hbm.1, bf16[1,2048,1792]{2,1,0:T(8,128)(2,1)} %wu_hbm.1, ...), custom_call_target="tpu_custom_call" | custom-call | tf_op jit(solution)/shard_map/pallas_call | solution.py:412
  88.4 2.3 %copy.12 = bf16[256,2048]{1,0:T(8,128)(2,1)} copy(bf16[256,2048]{1,0:T(8,128)(2,1)} %get-tuple-element.4) | data formatting | bytes 2097152
  90.7 1.3 %copy.13 = f32[1,1792]{1,0:T(1,128)} copy(f32[1,1792]{1,0:T(1,128)} %get-tuple-element.5) | data formatting | bytes 14336
